TPU v7x, 512 devices: a whole 4x4x16 slice. The times are simulated.
512 devices in a mesh: row: 32 (over y_lo, z), col: 16 (over y_hi, x, core).
Axes of the slice: x: 4, y: 4 (y_hi: 2, y_lo: 2; y = y_hi * 2 + y_lo), z: 16, core: 2. Of those that a mesh axis runs over, the one named last changes fastest.
Arguments:
- amplitudes: float32 [1280, 180224], P('row', 'col'), may hold values from -6 to 6
- integrals: float32 [768, 16, 32, 352], P(None, 'col', 'row'), may hold values from -0.013671875 to 0.013671875
Outputs:
- ladder: float32 [768, 1280], P('row', 'col')
All inputs are finite; a program needn't handle non-finite values.
Results may differ from a plain program's by a relative error of at most 0.000084.
Values sent between devices are 32-bit elements; how exact they have to be, the bound alone decides.
A program may use at most 64 MiB of HBM per device.

v0:
```python
import jax
import jax.numpy as jnp
from jax import lax
from jax.sharding import PartitionSpec as P


def contract(left, right):
    return lax.dot_general(
        left,
        right,
        (((1,), (1,)), ((), ())),
        precision=lax.Precision.HIGHEST,
        preferred_element_type=jnp.float32,
    )


def per_device(amplitudes, integrals):
    slab_rows = integrals.shape[0]
    piece_width = integrals.shape[3]
    regrouped = lax.all_to_all(amplitudes, "row", split_axis=1, concat_axis=0, tiled=True)
    panels = lax.all_to_all(regrouped, "col", split_axis=0, concat_axis=1, tiled=True)
    fragment = lax.all_gather(integrals, "col", axis=1, tiled=True)
    span_width = fragment.shape[1] * piece_width
    flattened = fragment.reshape(slab_rows, span_width)
    summed = contract(flattened, panels)
    return lax.psum_scatter(summed, "row", scatter_dimension=0, tiled=True)


def solution(mesh):
    return jax.shard_map(
        per_device,
        mesh=mesh,
        in_specs=(P("row", "col"), P(None, "col", "row", None)),
        out_specs=P("row", "col"),
        check_vma=False,
    )
```

profile of v0, /device:TPU:6, one launch (start us, length us, event | category | flops | bytes accessed | tf_op | source)
XLA Modules:
  0.0 347.7 jit_solution(16871820439174082074)
XLA Ops:
  6.5 0.0 all-gather.2.cloned.1.call-start
  6.5 0.7 all-gather.2.cloned.1.call-update
  7.3 0.0 reduce-scatter.5.cloned.1.call-start
  7.3 2.6 all_to_all.26
  10.0 1.1 copy.6
  11.1 107.6 %all_to_all.35 = f32[40,32,352]{2,0,1:T(8,128)S(1)} all-to-all(f32[40,32,352]{2,0,1:T(8,128)S(1)} %copy.6), channel_id=1, replica_groups=mesh['row'=32,'col'=16] {'row'}, dimensions={1} | all-to-all | bytes 3604480 | tf_op jit(solution)/shard_map/all_to_all | solution.py:20
  118.7 37.2 %all_to_all.36 = f32[16,80,352]{2,1,0:T(8,128)S(1)} all-to-all(f32[16,80,352]{2,1,0:T(8,128)S(1)} %bitcast.9), channel_id=1, replica_groups=mesh['row'=32,'col'=16] {'col'}, dimensions={0} | all-to-all | bytes 3604480 | tf_op jit(solution)/shard_map/all_to_all | solution.py:21
  155.9 0.6 copy.7
  156.6 2.2 all_to_all.32
  158.8 16.2 %all-gather.2.cloned.1.call-done = f32[768,16,1,352]{0,3,2,1:T(8,128)} async-done(((f32[768,1,1,352]{0,3,2,1:T(8,128)}), f32[768,16,1,352]{0,3,2,1:T(8,128)}) %all-gather.2.cloned.1.call-update) | async-done | bytes 17301520 | tf_op jit(solution)/shard_map/all_gather | solution.py:22
  175.0 31.1 %fusion = f32[768,80]{1,0:T(8,128)} fusion(f32[768,5632]{0,1:T(8,128)} %bitcast.8, f32[80,5632]{1,0:T(8,128)} %all_to_all.32), kind=kOutput, calls=%fused_computation | convolution fusion | flops 4152360960 | bytes 19349504 | tf_op jit(solution)/shard_map/dot_general | solution.py:8
  206.1 0.0 reduce-scatter.5.cloned.1.call-update
  206.1 134.7 %reduce-scatter.5.cloned.1.call-done = f32[24,80]{1,0:T(8,128)} async-done(((f32[768,80]{1,0:T(8,128)}), f32[24,80]{1,0:T(8,128)}) %reduce-scatter.5.cloned.1.call-update) | async-done | bytes 7696
Async XLA Ops:
  6.5 168.5 %all-gather.2.cloned.1.call-start = ((), (), s32[]{:S(2)}) async-start(), calls=%async_computation.3 | async-start | bytes 18382848 | tf_op jit(solution)/shard_map/all_gather | solution.py:22
  7.3 333.6 %reduce-scatter.5.cloned.1.call-start = ((), (), s32[]{:S(2)}) async-start(), calls=%async_computation.4 | async-start | bytes 405504
Sparse Core Ops, SparseCore 0:
  10.7 164.2 all-gather.1
  206.3 134.4 reduce-scatter.4
where the time goes:
time: 348 us
  waiting for transfers between devices  152 us (44%)
  blocking collectives  145 us (42%)
  matrix products  31.1 us (9%)
  between operations  13.4 us (4%)
  local copies, waits for them, and re-layouts  6.62 us (2%)
    unnamed x3, waiting for transfers between devices  135 us
    all_to_all x1, blocking collectives, per_device(): lax.all_to_all(amplitudes, 'row', split_axis=1, concat_axis=0, tiled=True)  108 us
    all_to_all x1, blocking collectives, per_device(): lax.all_to_all(regrouped, 'col', split_axis=0, concat_axis=1, tiled=True)  37.2 us
    dot_general x1, matrix products, contract(): lax.dot_general(left, right, (((1,), (1,)), ((), ())), precision=lax.Prec...  31.1 us
    all_gather x1, waiting for transfers between devices, per_device(): fragment = lax.all_gather(integrals, 'col', axis=1, tiled=True)  16.2 us
  transfers between devices with their start and end apart: 2, of which 2 were waited for; matrix products, arithmetic and copies ran while one was open for 1% of the time, Pallas kernels for 0%

commit v1 on v0

v1 whole, which is shorter than its diff:
```python
import jax
import jax.numpy as jnp
from jax import lax
from jax.experimental import pallas as pl
from jax.experimental.pallas import tpu as pltpu
from jax.sharding import PartitionSpec as P

MESH = pl.DeviceIdType.MESH
ROUNDS = 5
F32 = jnp.float32
BF16 = jnp.bfloat16


def wait_for(ref, sem):
    pltpu.make_async_copy(ref, ref, sem).wait()


def kernel(
    amp_hbm, int_hbm, out_ref,
    amp, ints, hi, lo, send_a, send_b, recv_a, recv_b,
    part, plane, near_out, near_in, total, far_out, far_in,
    load_sem, int_sem, send_sem, recv_sem, plane_send, plane_recv, near_send, near_recv, far_send, far_recv,
):
    row, col = lax.axis_index("row"), lax.axis_index("col")
    half, z = row // 16, row % 16
    z_hi, z_lo = z // 4, z % 4
    chip, core = col // 2, col % 2
    parity = (row // 2) % 2
    slot = (row // 4) * 2 + row % 2
    place = half * 8 + chip
    target = chip * 2 + parity
    mine = parity == core

    load_amp = pltpu.make_async_copy(amp_hbm, amp, load_sem.at[0])
    load_amp.start()
    load_int = pltpu.make_async_copy(int_hbm, ints.at[core], load_sem.at[1])
    load_int.start()

    def plane_peer(d):
        other = (place + d) % 16
        return other // 8, other % 8, ((other // 8) * 16 + z, (other % 8) * 2 + core)

    def near_peer(d):
        other = (z_lo + d) % 4
        return other, (half * 16 + z_hi * 4 + other, col)

    def far_peer(d):
        other = (z_hi + d) % 4
        return other, (half * 16 + other * 4 + z_lo, col)

    barrier = pltpu.get_barrier_semaphore()

    def greet(device):
        pl.semaphore_signal(barrier, inc=1, device_id=device, device_id_type=MESH)

    def greet_source(t, carry):
        source = (t // 4) * 4 + core * 2 + (t // 2) % 2
        source_col = chip * 2 + t % 2

        @pl.when(jnp.logical_or(source != row, source_col != col))
        def _():
            greet((source, source_col))

        return carry

    lax.fori_loop(0, 32, greet_source, 0)

    def greet_plane(d, carry):
        greet(plane_peer(16 - d)[2])
        return carry

    lax.fori_loop(1, 16, greet_plane, 0)
    for d in range(1, 4):
        greet(near_peer(4 - d)[1])
        greet(far_peer(4 - d)[1])
    greet((row, chip * 2 + 1 - core))

    load_amp.wait()

    def pack(g, carry):
        lane = lax.broadcasted_iota(jnp.int32, (40, 128), 1)
        lane8 = lax.broadcasted_iota(jnp.int32, (8, 128), 1)

        def load(t):
            return amp[:, pl.ds(pl.multiple_of(g * 1408 + t * 128, 128), 128)]

        for j in range(4):
            first, shift = (352 * j) // 128, (352 * j) % 128
            tiles = []
            for n in range(3):
                tile = load(first + n)
                if shift > 0:
                    tile = pltpu.roll(tile, 128 - shift, 1)
                    if first + n + 1 <= 10:
                        after = pltpu.roll(load(first + n + 1), 128 - shift, 1)
                        tile = jnp.where(lane < 128 - shift, tile, after)
                tiles.append(tile)
            dest = g * 4 + j
            for i in range(4):
                send_a[i, dest, 0] = tiles[0][8 * i:8 * i + 8]
                send_a[i, dest, 1] = tiles[1][8 * i:8 * i + 8]
                spare = pltpu.roll(tiles[2][32:40], 96 - 32 * i, 1) if i < 3 else jnp.zeros((8, 128), F32)
                send_a[i, dest, 2] = jnp.where(lane8 < 96, tiles[2][8 * i:8 * i + 8], spare)
            send_b[dest, 0] = tiles[0][32:40]
            send_b[dest, 1] = tiles[1][32:40]
        return carry

    lax.fori_loop(0, 8, pack, 0)
    load_int.wait()

    copies = jnp.where(mine, 31, 32)
    pl.semaphore_wait(barrier, copies + 15 + 3 + 3 + 1)

    sibling = pltpu.make_async_remote_copy(
        ints.at[core], ints.at[core], int_sem.at[0], int_sem.at[1],
        device_id=(row, chip * 2 + 1 - core), device_id_type=MESH,
    )
    sibling.start()

    def outgoing(i):
        return send_a.at[i] if i < 4 else send_b

    def incoming(i):
        return recv_a.at[i] if i < 4 else recv_b

    def send_round(i):
        src, dst = outgoing(i), incoming(i).at[core, slot]

        def send(t, carry):
            other = (row + t) % 32
            pltpu.make_async_remote_copy(
                src.at[other], dst, send_sem.at[i], recv_sem.at[i],
                device_id=(other, target), device_id_type=MESH,
            ).start()
            return carry

        lax.fori_loop(1, 32, send, 0)

        @pl.when(mine)
        def _():
            pltpu.make_async_copy(src.at[row], dst, recv_sem.at[i]).start()

        @pl.when(jnp.logical_not(mine))
        def _():
            pltpu.make_async_remote_copy(
                src.at[row], dst, send_sem.at[i], recv_sem.at[i],
                device_id=(row, target), device_id_type=MESH,
            ).start()

    send_round(0)
    send_round(1)

    sibling.wait()
    for c in range(2):
        whole = ints[c]
        upper = whole.astype(BF16)
        hi[384 * c:384 * c + 352] = upper
        lo[384 * c:384 * c + 352] = (whole - upper.astype(F32)).astype(BF16)
        hi[384 * c + 352:384 * c + 384] = jnp.zeros((32, 768), BF16)
        lo[384 * c + 352:384 * c + 384] = jnp.zeros((32, 768), BF16)

    def gathered(i):
        parts = []
        for c in range(2):
            if i < 4:
                parts += [recv_a[i, c, :, n].reshape(128, 128) for n in range(3)]
            else:
                lane = lax.broadcasted_iota(jnp.int32, (128, 128), 1)
                last = jnp.zeros((128, 128), F32)
                for g in range(3):
                    moved = pltpu.roll(recv_a[g, c, :, 2].reshape(128, 128), 32 + 32 * g, 1)
                    last = jnp.where(jnp.logical_and(lane >= 32 * g, lane < 32 * g + 32), moved, last)
                parts += [recv_b[c, :, n].reshape(128, 128) for n in range(2)] + [last]
        return jnp.concatenate(parts, axis=1)

    def product(i):
        left = gathered(i)
        upper = left.astype(BF16)
        lower = (left - upper.astype(F32)).astype(BF16)
        for h in range(2):
            lanes = slice(384 * h, 384 * h + 384)
            summed = jnp.dot(upper, lo[:, lanes], preferred_element_type=F32)
            summed += jnp.dot(lower, hi[:, lanes], preferred_element_type=F32)
            summed += jnp.dot(upper, hi[:, lanes], preferred_element_type=F32)
            part[i, h] = summed.reshape(8, 16, 384)

    def send_plane(i):
        def send(d, carry):
            other_half, other_chip, device = plane_peer(d)
            pltpu.make_async_remote_copy(
                part.at[i, other_half, other_chip], plane.at[i, d - 1], plane_send.at[i], plane_recv.at[i],
                device_id=device, device_id_type=MESH,
            ).start()
            return carry

        lax.fori_loop(1, 16, send, 0)

    def sum_plane(i):
        wait_for(plane.at[i], plane_recv.at[i])
        summed = part[i, half, chip]
        for d in range(15):
            summed = summed + plane[i, d]
        lane = lax.broadcasted_iota(jnp.int32, (16, 128), 1)
        for low in range(4):
            spread = jnp.zeros((16, 128), F32)
            for high in range(4):
                start = 24 * (4 * high + low)
                done = 0
                while done < 24:
                    tile, offset = (start + done) // 128, (start + done) % 128
                    count = min(24 - done, 128 - offset)
                    to = 32 * high + done
                    moved = summed[:, 128 * tile:128 * tile + 128]
                    if (to - offset) % 128:
                        moved = pltpu.roll(moved, (to - offset) % 128, 1)
                    spread = jnp.where(jnp.logical_and(lane >= to, lane < to + count), moved, spread)
                    done += count
            near_out[i, low] = spread
        for d in range(1, 4):
            other, device = near_peer(d)
            pltpu.make_async_remote_copy(
                near_out.at[i, other], near_in.at[i, d - 1], near_send.at[i, d - 1], near_recv.at[i, d - 1],
                device_id=device, device_id_type=MESH,
            ).start()

    def sum_near(i):
        summed = near_out[i, z_lo]
        for d in range(1, 4):
            wait_for(near_in.at[i, d - 1], near_recv.at[i, d - 1])
            summed = summed + near_in[i, d - 1]
        total[8 * i:8 * i + 8] = summed[0:8]
        total[40 + 8 * i:48 + 8 * i] = summed[8:16]

    total[80:128] = jnp.zeros((48, 128), F32)
    for i in range(ROUNDS):
        wait_for(incoming(i), recv_sem.at[i])
        if i + 2 < ROUNDS:
            send_round(i + 2)
        product(i)
        send_plane(i)
        if i >= 1:
            sum_plane(i - 1)
        if i >= 2:
            sum_near(i - 2)
    sum_near(ROUNDS - 2)
    sum_plane(ROUNDS - 1)
    sum_near(ROUNDS - 1)

    far_out[...] = total[...].T.reshape(4, 32, 128)
    for d in range(1, 4):
        other, device = far_peer(d)
        pltpu.make_async_remote_copy(
            far_out.at[other, pl.ds(0, 24)], far_in.at[d - 1], far_send.at[d - 1], far_recv.at[d - 1],
            device_id=device, device_id_type=MESH,
        ).start()
    summed = far_out[z_hi, 0:24]
    for d in range(1, 4):
        wait_for(far_in.at[d - 1], far_recv.at[d - 1])
        summed = summed + far_in[d - 1]
    out_ref[...] = summed[:, 0:80]

    for i in range(ROUNDS):
        @pl.when(mine)
        def _():
            wait_for(outgoing(i).at[pl.ds(0, 31)], send_sem.at[i])

        @pl.when(jnp.logical_not(mine))
        def _():
            wait_for(outgoing(i), send_sem.at[i])

        wait_for(plane.at[i], plane_send.at[i])
        for d in range(3):
            wait_for(near_in.at[i, d], near_send.at[i, d])
    for d in range(3):
        wait_for(far_in.at[d], far_send.at[d])


def per_device(amplitudes, integrals):
    flat = integrals.reshape(768, 352).T
    dma = pltpu.SemaphoreType.DMA
    return pl.pallas_call(
        kernel,
        out_shape=jax.ShapeDtypeStruct((24, 80), F32),
        in_specs=[pl.BlockSpec(memory_space=pl.ANY)] * 2,
        out_specs=pl.BlockSpec(memory_space=pltpu.VMEM),
        scratch_shapes=[
            pltpu.VMEM((40, 11264), F32),
            pltpu.VMEM((2, 352, 768), F32),
            pltpu.VMEM((768, 768), BF16),
            pltpu.VMEM((768, 768), BF16),
            pltpu.VMEM((4, 32, 3, 8, 128), F32),
            pltpu.VMEM((32, 2, 8, 128), F32),
            pltpu.VMEM((4, 2, 16, 3, 8, 128), F32),
            pltpu.VMEM((2, 16, 2, 8, 128), F32),
            pltpu.VMEM((ROUNDS, 2, 8, 16, 384), F32),
            pltpu.VMEM((ROUNDS, 15, 16, 384), F32),
            pltpu.VMEM((ROUNDS, 4, 16, 128), F32),
            pltpu.VMEM((ROUNDS, 3, 16, 128), F32),
            pltpu.VMEM((128, 128), F32),
            pltpu.VMEM((4, 32, 128), F32),
            pltpu.VMEM((3, 24, 128), F32),
            dma((2,)),
            dma((2,)),
            dma((ROUNDS,)),
            dma((ROUNDS,)),
            dma((ROUNDS,)),
            dma((ROUNDS,)),
            dma((ROUNDS, 3)),
            dma((ROUNDS, 3)),
            dma((3,)),
            dma((3,)),
        ],
        compiler_params=pltpu.CompilerParams(
            collective_id=0, has_side_effects=True, vmem_limit_bytes=40 << 20
        ),
    )(amplitudes, flat)


def solution(mesh):
    return jax.shard_map(
        per_device,
        mesh=mesh,
        in_specs=(P("row", "col"), P(None, "col", "row", None)),
        out_specs=P("row", "col"),
        check_vma=False,
    )
```

time: 348 us -> 125 us (0.36)
  waiting for transfers between devices: 152 us -> 0 us
  blocking collectives: 145 us -> 0 us
  Pallas kernels: 0 us -> 121 us
  matrix products: 31.1 us -> 0 us
  between operations: 13.4 us -> 0.01 us
    all_to_all x2 -> x0, blocking collectives: 145 us -> none  [the longest x1 108 us: per_device(): lax.all_to_all(amplitudes, 'row', split_axis=1, concat_axis=0, tiled=True)]
    unnamed x3 -> x0, waiting for transfers between devices: 135 us -> none
    pallas_call x0 -> x1, Pallas kernels: none -> 121 us  [per_device(): pl.pallas_call(kernel, out_shape=jax.ShapeDtypeStruct((24, 80), F32), in_...]
    dot_general x1 -> x0, matrix products: 31.1 us -> none  [contract(): lax.dot_general(left, right, (((1,), (1,)), ((), ())), precision=lax.Prec...]
    all_gather x1 -> x0, waiting for transfers between devices: 16.2 us -> none  [per_device(): fragment = lax.all_gather(integrals, 'col', axis=1, tiled=True)]
    all_to_all x4 -> x0, local copies, waits for them, and re-layouts: 6.62 us -> none  [the longest x2 3.79 us: per_device(): lax.all_to_all(amplitudes, 'row', split_axis=1, concat_axis=0, tiled=True)]
  transfers between devices with their start and end apart: 2 -> 0, of which waited for: 2 -> 0; matrix products, arithmetic and copies ran while one was open for 1% -> 0% of each run, Pallas kernels for 0% -> 0%
where the time goes in v1:
time: 125 us
  Pallas kernels  121 us (97%)
  local copies, waits for them, and re-layouts  3.33 us (3%)
    pallas_call x1, Pallas kernels, per_device(): pl.pallas_call(kernel, out_shape=jax.ShapeDtypeStruct((24, 80), F32), in_...  121 us
    unnamed x5, local copies, waits for them, and re-layouts  3.33 us

profile of v1, /device:TPU:6, one launch (start us, length us, event | category | flops | bytes accessed | tf_op | source)
XLA Modules:
  0.0 124.7 jit_solution(9400652510112641050)
XLA Ops:
  0.0 0.0 copy-start
  0.0 1.5 %copy-done = f32[40,11264]{1,0:T(8,128)S(1)} copy-done((f32[40,11264]{1,0:T(8,128)S(1)}, f32[40,11264]{1,0:T(8,128)}, u32[]{:S(2)}) %copy-start) | copy-done | bytes 1802264
  1.5 0.0 copy-start.1
  1.5 1.2 copy-done.1
  2.7 121.4 %shard_map.28 = f32[24,80]{1,0:T(8,128)S(1)} custom-call(f32[40,11264]{1,0:T(8,128)S(1)} %copy-done, f32[352,768]{1,0:T(8,128)S(1)} %bitcast.3), custom_call_target="tpu_custom_call" | custom-call | tf_op jit(solution)/shard_map/pallas_call | solution.py:281
  124.1 0.6 copy.4
Async XLA Ops:
  0.0 1.5 %copy-start = (f32[40,11264]{1,0:T(8,128)S(1)}, f32[40,11264]{1,0:T(8,128)}, u32[]{:S(2)}) copy-start(f32[40,11264]{1,0:T(8,128)} %amp_hbm.1) | copy-start | bytes 5406724
  1.5 1.2 copy-start.1

commit v2 on v1

--- a/solution.py
+++ b/solution.py
@@ -6,7 +6,7 @@
 from jax.sharding import PartitionSpec as P
 
 MESH = pl.DeviceIdType.MESH
-ROUNDS = 5
+ROUNDS = 6
 F32 = jnp.float32
 BF16 = jnp.bfloat16
 
@@ -18,8 +18,9 @@
 def kernel(
     amp_hbm, int_hbm, out_ref,
     amp, ints, hi, lo, send_a, send_b, recv_a, recv_b,
-    part, plane, near_out, near_in, total, far_out, far_in,
+    part_a, part_b, plane_a, plane_b, near_out_a, near_out_b, near_in_a, near_in_b, total, turned, far_out, far_in, last_in,
     load_sem, int_sem, send_sem, recv_sem, plane_send, plane_recv, near_send, near_recv, far_send, far_recv,
+    last_send, last_recv,
 ):
     row, col = lax.axis_index("row"), lax.axis_index("col")
     half, z = row // 16, row % 16
@@ -48,6 +49,10 @@
         other = (z_hi + d) % 4
         return other, (half * 16 + other * 4 + z_lo, col)
 
+    def z_peer(d):
+        other = (z + d) % 16
+        return other, (half * 16 + other, col)
+
     barrier = pltpu.get_barrier_semaphore()
 
     def greet(device):
@@ -69,10 +74,12 @@
         greet(plane_peer(16 - d)[2])
         return carry
 
+    def greet_z(d, carry):
+        greet(z_peer(16 - d)[1])
+        return carry
+
     lax.fori_loop(1, 16, greet_plane, 0)
-    for d in range(1, 4):
-        greet(near_peer(4 - d)[1])
-        greet(far_peer(4 - d)[1])
+    lax.fori_loop(1, 16, greet_z, 0)
     greet((row, chip * 2 + 1 - core))
 
     load_amp.wait()
@@ -80,6 +87,7 @@
     def pack(g, carry):
         lane = lax.broadcasted_iota(jnp.int32, (40, 128), 1)
         lane8 = lax.broadcasted_iota(jnp.int32, (8, 128), 1)
+        sub8 = lax.broadcasted_iota(jnp.int32, (8, 128), 0)
 
         def load(t):
             return amp[:, pl.ds(pl.multiple_of(g * 1408 + t * 128, 128), 128)]
@@ -101,15 +109,16 @@
                 send_a[i, dest, 1] = tiles[1][8 * i:8 * i + 8]
                 spare = pltpu.roll(tiles[2][32:40], 96 - 32 * i, 1) if i < 3 else jnp.zeros((8, 128), F32)
                 send_a[i, dest, 2] = jnp.where(lane8 < 96, tiles[2][8 * i:8 * i + 8], spare)
-            send_b[dest, 0] = tiles[0][32:40]
-            send_b[dest, 1] = tiles[1][32:40]
+            first8, second8 = tiles[0][32:40], tiles[1][32:40]
+            send_b[0, dest] = jnp.where(sub8 < 4, first8, pltpu.roll(second8, 4, 0))
+            send_b[1, dest] = jnp.where(sub8 < 4, pltpu.roll(first8, 4, 0), second8)
         return carry
 
     lax.fori_loop(0, 8, pack, 0)
     load_int.wait()
 
     copies = jnp.where(mine, 31, 32)
-    pl.semaphore_wait(barrier, copies + 15 + 3 + 3 + 1)
+    pl.semaphore_wait(barrier, copies + 15 + 15 + 1)
 
     sibling = pltpu.make_async_remote_copy(
         ints.at[core], ints.at[core], int_sem.at[0], int_sem.at[1],
@@ -118,10 +127,22 @@
     sibling.start()
 
     def outgoing(i):
-        return send_a.at[i] if i < 4 else send_b
+        return send_a.at[i] if i < 4 else send_b.at[i - 4]
 
     def incoming(i):
-        return recv_a.at[i] if i < 4 else recv_b
+        return recv_a.at[i] if i < 4 else recv_b.at[i - 4]
+
+    def part(i):
+        return part_a.at[i] if i < 4 else part_b.at[i - 4]
+
+    def plane(i):
+        return plane_a.at[i] if i < 4 else plane_b.at[i - 4]
+
+    def near_out(i):
+        return near_out_a.at[i] if i < 4 else near_out_b.at[i - 4]
+
+    def near_in(i):
+        return near_in_a.at[i] if i < 4 else near_in_b
 
     def send_round(i):
         src, dst = outgoing(i), incoming(i).at[core, slot]
@@ -160,17 +181,34 @@
         lo[384 * c + 352:384 * c + 384] = jnp.zeros((32, 768), BF16)
 
     def gathered(i):
+        if i < 4:
+            return jnp.concatenate(
+                [recv_a[i, c, :, n].reshape(128, 128) for c in range(2) for n in range(3)], axis=1
+            )
+        sub = lax.broadcasted_iota(jnp.int32, (64, 128), 0) % 8
+        lane = lax.broadcasted_iota(jnp.int32, (64, 128), 1)
+
+        def evens_odds(ref):
+            whole = ref.reshape(8, 2, 8, 128)
+            return whole[:, 0].reshape(64, 128), whole[:, 1].reshape(64, 128)
+
+        def upper_rows(even, odd):
+            return jnp.where(sub < 4, even, pltpu.roll(odd, 4, 0))
+
+        def lower_rows(even, odd):
+            return jnp.where(sub < 4, pltpu.roll(even, 60, 0), odd)
+
         parts = []
         for c in range(2):
-            if i < 4:
-                parts += [recv_a[i, c, :, n].reshape(128, 128) for n in range(3)]
-            else:
-                lane = lax.broadcasted_iota(jnp.int32, (128, 128), 1)
-                last = jnp.zeros((128, 128), F32)
-                for g in range(3):
-                    moved = pltpu.roll(recv_a[g, c, :, 2].reshape(128, 128), 32 + 32 * g, 1)
-                    last = jnp.where(jnp.logical_and(lane >= 32 * g, lane < 32 * g + 32), moved, last)
-                parts += [recv_b[c, :, n].reshape(128, 128) for n in range(2)] + [last]
+            even, odd = evens_odds(recv_b[i - 4, c])
+            parts += [upper_rows(even, odd), lower_rows(even, odd)]
+            last = jnp.zeros((64, 128), F32)
+            for g in range(3):
+                even, odd = evens_odds(recv_a[g, c, :, 2])
+                merged = upper_rows(even, odd) if i == 4 else lower_rows(even, odd)
+                moved = pltpu.roll(merged, 32 + 32 * g, 1)
+                last = jnp.where(jnp.logical_and(lane >= 32 * g, lane < 32 * g + 32), moved, last)
+            parts.append(last)
         return jnp.concatenate(parts, axis=1)
 
     def product(i):
@@ -182,13 +220,13 @@
             summed = jnp.dot(upper, lo[:, lanes], preferred_element_type=F32)
             summed += jnp.dot(lower, hi[:, lanes], preferred_element_type=F32)
             summed += jnp.dot(upper, hi[:, lanes], preferred_element_type=F32)
-            part[i, h] = summed.reshape(8, 16, 384)
+            part(i)[h] = summed.reshape(8, 16 if i < 4 else 8, 384)
 
     def send_plane(i):
         def send(d, carry):
             other_half, other_chip, device = plane_peer(d)
             pltpu.make_async_remote_copy(
-                part.at[i, other_half, other_chip], plane.at[i, d - 1], plane_send.at[i], plane_recv.at[i],
+                part(i).at[other_half, other_chip], plane(i).at[d - 1], plane_send.at[i], plane_recv.at[i],
                 device_id=device, device_id_type=MESH,
             ).start()
             return carry
@@ -196,13 +234,14 @@
         lax.fori_loop(1, 16, send, 0)
 
     def sum_plane(i):
-        wait_for(plane.at[i], plane_recv.at[i])
-        summed = part[i, half, chip]
+        wait_for(plane(i), plane_recv.at[i])
+        summed = part(i)[half, chip]
         for d in range(15):
-            summed = summed + plane[i, d]
-        lane = lax.broadcasted_iota(jnp.int32, (16, 128), 1)
+            summed = summed + plane(i)[d]
+        rows = summed.shape[0]
+        lane = lax.broadcasted_iota(jnp.int32, (rows, 128), 1)
         for low in range(4):
-            spread = jnp.zeros((16, 128), F32)
+            spread = jnp.zeros((rows, 128), F32)
             for high in range(4):
                 start = 24 * (4 * high + low)
                 done = 0
@@ -215,21 +254,28 @@
                         moved = pltpu.roll(moved, (to - offset) % 128, 1)
                     spread = jnp.where(jnp.logical_and(lane >= to, lane < to + count), moved, spread)
                     done += count
-            near_out[i, low] = spread
+            near_out(i)[low] = spread
+
+    def send_near(i):
         for d in range(1, 4):
             other, device = near_peer(d)
             pltpu.make_async_remote_copy(
-                near_out.at[i, other], near_in.at[i, d - 1], near_send.at[i, d - 1], near_recv.at[i, d - 1],
+                near_out(i).at[other], near_in(i).at[d - 1], near_send.at[i, d - 1], near_recv.at[i, d - 1],
                 device_id=device, device_id_type=MESH,
             ).start()
 
     def sum_near(i):
-        summed = near_out[i, z_lo]
+        summed = near_out(i)[z_lo]
         for d in range(1, 4):
-            wait_for(near_in.at[i, d - 1], near_recv.at[i, d - 1])
-            summed = summed + near_in[i, d - 1]
-        total[8 * i:8 * i + 8] = summed[0:8]
-        total[40 + 8 * i:48 + 8 * i] = summed[8:16]
+            wait_for(near_in(i).at[d - 1], near_recv.at[i, d - 1])
+            summed = summed + near_in(i)[d - 1]
+        if i < 4:
+            total[8 * i:8 * i + 8] = summed[0:8]
+            total[40 + 8 * i:48 + 8 * i] = summed[8:16]
+        else:
+            sub = lax.broadcasted_iota(jnp.int32, (8, 128), 0)
+            total[32:40] = jnp.where(sub < 4, summed, 0.0)
+            total[72:80] = jnp.where(sub < 4, pltpu.roll(summed, 4, 0), 0.0)
 
     total[80:128] = jnp.zeros((48, 128), F32)
     for i in range(ROUNDS):
@@ -240,11 +286,10 @@
         send_plane(i)
         if i >= 1:
             sum_plane(i - 1)
+            send_near(i - 1)
         if i >= 2:
             sum_near(i - 2)
     sum_near(ROUNDS - 2)
-    sum_plane(ROUNDS - 1)
-    sum_near(ROUNDS - 1)
 
     far_out[...] = total[...].T.reshape(4, 32, 128)
     for d in range(1, 4):
@@ -253,11 +298,34 @@
             far_out.at[other, pl.ds(0, 24)], far_in.at[d - 1], far_send.at[d - 1], far_recv.at[d - 1],
             device_id=device, device_id_type=MESH,
         ).start()
+
+    sum_plane(ROUNDS - 1)
+
+    def send_last(d, carry):
+        other, device = z_peer(d)
+        pltpu.make_async_remote_copy(
+            near_out_b.at[1, other % 4], last_in.at[d - 1], last_send, last_recv,
+            device_id=device, device_id_type=MESH,
+        ).start()
+        return carry
+
+    lax.fori_loop(1, 16, send_last, 0)
     summed = far_out[z_hi, 0:24]
     for d in range(1, 4):
         wait_for(far_in.at[d - 1], far_recv.at[d - 1])
         summed = summed + far_in[d - 1]
-    out_ref[...] = summed[:, 0:80]
+
+    wait_for(last_in, last_recv)
+    last = near_out_b[1, z_lo]
+    for d in range(15):
+        last = last + last_in[d]
+    sub = lax.broadcasted_iota(jnp.int32, (8, 128), 0)
+    total[0:32] = jnp.zeros((32, 128), F32)
+    total[32:40] = jnp.where(sub < 4, 0.0, pltpu.roll(last, 4, 0))
+    total[40:72] = jnp.zeros((32, 128), F32)
+    total[72:80] = jnp.where(sub < 4, 0.0, last)
+    turned[...] = total[...].T.reshape(4, 32, 128)
+    out_ref[...] = (summed + turned[z_hi, 0:24])[:, 0:80]
 
     for i in range(ROUNDS):
         @pl.when(mine)
@@ -268,11 +336,13 @@
         def _():
             wait_for(outgoing(i), send_sem.at[i])
 
-        wait_for(plane.at[i], plane_send.at[i])
-        for d in range(3):
-            wait_for(near_in.at[i, d], near_send.at[i, d])
+        wait_for(plane(i), plane_send.at[i])
+        if i < ROUNDS - 1:
+            for d in range(3):
+                wait_for(near_in(i).at[d], near_send.at[i, d])
     for d in range(3):
         wait_for(far_in.at[d], far_send.at[d])
+    wait_for(last_in, last_send)
 
 
 def per_device(amplitudes, integrals):
@@ -289,16 +359,22 @@
             pltpu.VMEM((768, 768), BF16),
             pltpu.VMEM((768, 768), BF16),
             pltpu.VMEM((4, 32, 3, 8, 128), F32),
-            pltpu.VMEM((32, 2, 8, 128), F32),
+            pltpu.VMEM((2, 32, 8, 128), F32),
             pltpu.VMEM((4, 2, 16, 3, 8, 128), F32),
-            pltpu.VMEM((2, 16, 2, 8, 128), F32),
-            pltpu.VMEM((ROUNDS, 2, 8, 16, 384), F32),
-            pltpu.VMEM((ROUNDS, 15, 16, 384), F32),
-            pltpu.VMEM((ROUNDS, 4, 16, 128), F32),
-            pltpu.VMEM((ROUNDS, 3, 16, 128), F32),
+            pltpu.VMEM((2, 2, 16, 8, 128), F32),
+            pltpu.VMEM((4, 2, 8, 16, 384), F32),
+            pltpu.VMEM((2, 2, 8, 8, 384), F32),
+            pltpu.VMEM((4, 15, 16, 384), F32),
+            pltpu.VMEM((2, 15, 8, 384), F32),
+            pltpu.VMEM((4, 4, 16, 128), F32),
+            pltpu.VMEM((2, 4, 8, 128), F32),
+            pltpu.VMEM((4, 3, 16, 128), F32),
+            pltpu.VMEM((3, 8, 128), F32),
             pltpu.VMEM((128, 128), F32),
             pltpu.VMEM((4, 32, 128), F32),
+            pltpu.VMEM((4, 32, 128), F32),
             pltpu.VMEM((3, 24, 128), F32),
+            pltpu.VMEM((15, 8, 128), F32),
             dma((2,)),
             dma((2,)),
             dma((ROUNDS,)),
@@ -309,9 +385,11 @@
             dma((ROUNDS, 3)),
             dma((3,)),
             dma((3,)),
+            dma,
+            dma,
         ],
         compiler_params=pltpu.CompilerParams(
-            collective_id=0, has_side_effects=True, vmem_limit_bytes=40 << 20
+            collective_id=0, has_side_effects=True, vmem_limit_bytes=60 << 20
         ),
     )(amplitudes, flat)
 

time: 125 us -> 122 us (0.976)
  local copies, waits for them, and re-layouts: 3.33 us -> 1.31 us
    unnamed x5 -> x1, local copies, waits for them, and re-layouts: 3.33 us -> 1.31 us
    pallas_call x1, Pallas kernels: 121 us -> 120 us  [per_device(): pl.pallas_call(kernel, out_shape=jax.ShapeDtypeStruct((24, 80), F32), in_...]
where the time goes in v2:
time: 122 us; the launch traced here: 121 us
  Pallas kernels  120 us (98%)
  local copies, waits for them, and re-layouts  1.31 us (1%)
    pallas_call x1, Pallas kernels, per_device(): pl.pallas_call(kernel, out_shape=jax.ShapeDtypeStruct((24, 80), F32), in_...  120 us

profile of v2, /device:TPU:6, one launch (start us, length us, event | category | flops | bytes accessed | tf_op | source)
XLA Modules:
  0.0 121.0 jit_solution(15565860322024776417)
XLA Ops:
  0.0 119.7 %shard_map.28 = f32[24,80]{1,0:T(8,128)} custom-call(f32[40,11264]{1,0:T(8,128)} %amp_hbm.1, f32[352,768]{1,0:T(8,128)} %bitcast.3), custom_call_target="tpu_custom_call" | custom-call | tf_op jit(solution)/shard_map/pallas_call | solution.py:351
  119.7 1.3 %copy.4 = f32[24,80]{1,0:T(8,128)} copy(f32[24,80]{1,0:T(8,128)} %shard_map.28) | data formatting | bytes 15360

commit v3 on v2

--- a/solution.py
+++ b/solution.py
@@ -18,7 +18,7 @@
 def kernel(
     amp_hbm, int_hbm, out_ref,
     amp, ints, hi, lo, send_a, send_b, recv_a, recv_b,
-    part_a, part_b, plane_a, plane_b, near_out_a, near_out_b, near_in_a, near_in_b, total, turned, far_out, far_in, last_in,
+    part_a, part_b, plane_a, plane_b, near_out_a, near_out_b, near_in, total, turned, far_out, far_in, last_in,
     load_sem, int_sem, send_sem, recv_sem, plane_send, plane_recv, near_send, near_recv, far_send, far_recv,
     last_send, last_recv,
 ):
@@ -141,21 +141,20 @@
     def near_out(i):
         return near_out_a.at[i] if i < 4 else near_out_b.at[i - 4]
 
-    def near_in(i):
-        return near_in_a.at[i] if i < 4 else near_in_b
-
     def send_round(i):
         src, dst = outgoing(i), incoming(i).at[core, slot]
 
         def send(t, carry):
-            other = (row + t) % 32
+            k = t // 2
+            dz = jnp.where(k % 2 == 1, 8 - (k + 1) // 2, 8 + k // 2)
+            other = ((half + t + 1) % 2) * 16 + (z + dz) % 16
             pltpu.make_async_remote_copy(
                 src.at[other], dst, send_sem.at[i], recv_sem.at[i],
                 device_id=(other, target), device_id_type=MESH,
             ).start()
             return carry
 
-        lax.fori_loop(1, 32, send, 0)
+        lax.fori_loop(0, 31, send, 0)
 
         @pl.when(mine)
         def _():
@@ -168,8 +167,8 @@
                 device_id=(row, target), device_id_type=MESH,
             ).start()
 
-    send_round(0)
-    send_round(1)
+    for i in range(3):
+        send_round(i)
 
     sibling.wait()
     for c in range(2):
@@ -260,36 +259,52 @@
         for d in range(1, 4):
             other, device = near_peer(d)
             pltpu.make_async_remote_copy(
-                near_out(i).at[other], near_in(i).at[d - 1], near_send.at[i, d - 1], near_recv.at[i, d - 1],
+                near_out_a.at[i, other], near_in.at[i, d - 1], near_send.at[i, d - 1], near_recv.at[i, d - 1],
                 device_id=device, device_id_type=MESH,
             ).start()
 
     def sum_near(i):
-        summed = near_out(i)[z_lo]
+        summed = near_out_a[i, z_lo]
         for d in range(1, 4):
-            wait_for(near_in(i).at[d - 1], near_recv.at[i, d - 1])
-            summed = summed + near_in(i)[d - 1]
-        if i < 4:
-            total[8 * i:8 * i + 8] = summed[0:8]
-            total[40 + 8 * i:48 + 8 * i] = summed[8:16]
-        else:
-            sub = lax.broadcasted_iota(jnp.int32, (8, 128), 0)
-            total[32:40] = jnp.where(sub < 4, summed, 0.0)
-            total[72:80] = jnp.where(sub < 4, pltpu.roll(summed, 4, 0), 0.0)
-
-    total[80:128] = jnp.zeros((48, 128), F32)
+            wait_for(near_in.at[i, d - 1], near_recv.at[i, d - 1])
+            summed = summed + near_in[i, d - 1]
+        total[8 * i:8 * i + 8] = summed[0:8]
+        total[40 + 8 * i:48 + 8 * i] = summed[8:16]
+
+    def send_last(i):
+        def send(d, carry):
+            other, device = z_peer(d)
+            pltpu.make_async_remote_copy(
+                near_out_b.at[i - 4, other % 4], last_in.at[i - 4, d - 1], last_send.at[i - 4], last_recv.at[i - 4],
+                device_id=device, device_id_type=MESH,
+            ).start()
+            return carry
+
+        lax.fori_loop(1, 16, send, 0)
+
+    def sum_last(i):
+        wait_for(last_in.at[i - 4], last_recv.at[i - 4])
+        summed = near_out_b[i - 4, z_lo]
+        for d in range(15):
+            summed = summed + last_in[i - 4, d]
+        return summed
+
+    for rows in (slice(32, 40), slice(72, 128)):
+        total[rows] = jnp.zeros((rows.stop - rows.start, 128), F32)
     for i in range(ROUNDS):
         wait_for(incoming(i), recv_sem.at[i])
-        if i + 2 < ROUNDS:
-            send_round(i + 2)
+        if i + 3 < ROUNDS:
+            send_round(i + 3)
         product(i)
         send_plane(i)
         if i >= 1:
             sum_plane(i - 1)
-            send_near(i - 1)
+            if i <= 4:
+                send_near(i - 1)
+            else:
+                send_last(i - 1)
         if i >= 2:
             sum_near(i - 2)
-    sum_near(ROUNDS - 2)
 
     far_out[...] = total[...].T.reshape(4, 32, 128)
     for d in range(1, 4):
@@ -300,30 +315,19 @@
         ).start()
 
     sum_plane(ROUNDS - 1)
-
-    def send_last(d, carry):
-        other, device = z_peer(d)
-        pltpu.make_async_remote_copy(
-            near_out_b.at[1, other % 4], last_in.at[d - 1], last_send, last_recv,
-            device_id=device, device_id_type=MESH,
-        ).start()
-        return carry
-
-    lax.fori_loop(1, 16, send_last, 0)
+    send_last(ROUNDS - 1)
+
     summed = far_out[z_hi, 0:24]
     for d in range(1, 4):
         wait_for(far_in.at[d - 1], far_recv.at[d - 1])
         summed = summed + far_in[d - 1]
 
-    wait_for(last_in, last_recv)
-    last = near_out_b[1, z_lo]
-    for d in range(15):
-        last = last + last_in[d]
+    for rows in (slice(0, 32), slice(40, 72)):
+        total[rows] = jnp.zeros((32, 128), F32)
     sub = lax.broadcasted_iota(jnp.int32, (8, 128), 0)
-    total[0:32] = jnp.zeros((32, 128), F32)
-    total[32:40] = jnp.where(sub < 4, 0.0, pltpu.roll(last, 4, 0))
-    total[40:72] = jnp.zeros((32, 128), F32)
-    total[72:80] = jnp.where(sub < 4, 0.0, last)
+    fourth, fifth = sum_last(4), sum_last(5)
+    total[32:40] = jnp.where(sub < 4, fourth, pltpu.roll(fifth, 4, 0))
+    total[72:80] = jnp.where(sub < 4, pltpu.roll(fourth, 4, 0), fifth)
     turned[...] = total[...].T.reshape(4, 32, 128)
     out_ref[...] = (summed + turned[z_hi, 0:24])[:, 0:80]
 
@@ -337,12 +341,13 @@
             wait_for(outgoing(i), send_sem.at[i])
 
         wait_for(plane(i), plane_send.at[i])
-        if i < ROUNDS - 1:
+        if i < 4:
             for d in range(3):
-                wait_for(near_in(i).at[d], near_send.at[i, d])
+                wait_for(near_in.at[i, d], near_send.at[i, d])
+        else:
+            wait_for(last_in.at[i - 4], last_send.at[i - 4])
     for d in range(3):
         wait_for(far_in.at[d], far_send.at[d])
-    wait_for(last_in, last_send)
 
 
 def per_device(amplitudes, integrals):
@@ -369,24 +374,23 @@
             pltpu.VMEM((4, 4, 16, 128), F32),
             pltpu.VMEM((2, 4, 8, 128), F32),
             pltpu.VMEM((4, 3, 16, 128), F32),
-            pltpu.VMEM((3, 8, 128), F32),
             pltpu.VMEM((128, 128), F32),
             pltpu.VMEM((4, 32, 128), F32),
             pltpu.VMEM((4, 32, 128), F32),
             pltpu.VMEM((3, 24, 128), F32),
-            pltpu.VMEM((15, 8, 128), F32),
+            pltpu.VMEM((2, 15, 8, 128), F32),
             dma((2,)),
             dma((2,)),
             dma((ROUNDS,)),
             dma((ROUNDS,)),
             dma((ROUNDS,)),
             dma((ROUNDS,)),
-            dma((ROUNDS, 3)),
-            dma((ROUNDS, 3)),
+            dma((4, 3)),
+            dma((4, 3)),
             dma((3,)),
             dma((3,)),
-            dma,
-            dma,
+            dma((2,)),
+            dma((2,)),
         ],
         compiler_params=pltpu.CompilerParams(
             collective_id=0, has_side_effects=True, vmem_limit_bytes=60 << 20

time: 122 us -> 119 us (0.975)
  Pallas kernels: 120 us -> 117 us
    pallas_call x1, Pallas kernels: 120 us -> 117 us  [per_device(): pl.pallas_call(kernel, out_shape=jax.ShapeDtypeStruct((24, 80), F32), in_...]
where the time goes in v3:
time: 119 us; the launch traced here: 118 us
  Pallas kernels  117 us (98%)
  local copies, waits for them, and re-layouts  1.31 us (1%)
    pallas_call x1, Pallas kernels, per_device(): pl.pallas_call(kernel, out_shape=jax.ShapeDtypeStruct((24, 80), F32), in_...  117 us

profile of v3, /device:TPU:6, one launch (start us, length us, event | category | flops | bytes accessed | tf_op | source)
XLA Modules:
  0.0 118.2 jit_solution(9744624649708787385)
XLA Ops:
  0.0 116.9 %shard_map.28 = f32[24,80]{1,0:T(8,128)} custom-call(f32[40,11264]{1,0:T(8,128)} %amp_hbm.1, f32[352,768]{1,0:T(8,128)} %bitcast.3), custom_call_target="tpu_custom_call" | custom-call | tf_op jit(solution)/shard_map/pallas_call | solution.py:356
  116.9 1.3 %copy.4 = f32[24,80]{1,0:T(8,128)} copy(f32[24,80]{1,0:T(8,128)} %shard_map.28) | data formatting | bytes 15360
